TPU v7x, 256 devices: a whole 4x4x8 slice. The times are simulated.
256 devices in a mesh: dp: 32 (over z_hi, x, core), fsdp: 8 (over z_lo, y).
Axes of the slice: x: 4, y: 4, z: 8 (z_hi: 4, z_lo: 2; z = z_hi * 2 + z_lo), core: 2. Of those that a mesh axis runs over, the one named last changes fastest.
Arguments:
- hidden: bfloat16 [256, 2, 256, 8192], P(('dp', 'fsdp')), may hold values from -6 to 6
- frozen_weight: bfloat16 [8192, 1024], P('fsdp'), may hold values from -0.0625 to 0.0625
- adapter_down_weight: bfloat16 [8192, 128], P('fsdp'), may hold values from -0.0625 to 0.0625
- adapter_up_weight: bfloat16 [2, 64, 512], replicated, may hold values from -0.75 to 0.75
- readout: bfloat16 [256, 2, 256, 512], P(('dp', 'fsdp')), may hold values from -0.25 to 0.25
- chosen: int32 [256], P(('dp', 'fsdp')), may hold values from 0 to 1
- response_length: int32 [256, 2], P(('dp', 'fsdp')), may hold values from 64 to 256, as said below
Outputs:
- grad_down: float32 [8192, 128], P('fsdp')
- grad_up: float32 [2, 64, 512], replicated
Inputs may be any that keep to these rules, and one draw needn't show every extreme that they name: `chosen`: 0 names the first sequence of the pair, 1 the second. A sequence's response is its last response_length positions.
All inputs are finite; a program needn't handle non-finite values.
Results may differ from a plain program's by a relative error of at most 0.006.
Values may be sent and summed in bfloat16 or wider, within the bound.
A program may use at most 128 MiB of HBM per device.

v0:
```python
import jax
import jax.numpy as jnp
from jax import lax
from jax.sharding import PartitionSpec as P

adapter_scale = 0.5
preference_beta = 0.1


def local(
    hidden, frozen_weight, adapter_down_weight, adapter_up_weight, readout, chosen, response_length
):
    pair_count, two_seqs, positions, model_width = hidden.shape
    adapter_rank_columns = adapter_up_weight.shape[1]
    key_value_columns = adapter_up_weight.shape[2]
    token_count = pair_count * two_seqs * positions
    token_row_block = hidden.reshape(token_count, model_width)
    columns = token_row_block
    base_out = jnp.dot(
        columns,
        lax.all_gather(frozen_weight, "fsdp", axis=0, tiled=True),
        preferred_element_type=jnp.float32,
    )
    lowered_full = jnp.dot(
        columns,
        lax.all_gather(adapter_down_weight, "fsdp", axis=0, tiled=True),
        preferred_element_type=jnp.float32,
    )
    projected_rows = lowered_full.astype(jnp.bfloat16)
    reference_keys = base_out[:, :key_value_columns]
    reference_values = base_out[:, key_value_columns:]
    projected_keys = projected_rows[:, :adapter_rank_columns]
    projected_values = projected_rows[:, adapter_rank_columns:]
    policy_keys = reference_keys + adapter_scale * jnp.dot(
        projected_keys, adapter_up_weight[0], preferred_element_type=jnp.float32
    )
    policy_values = reference_values + adapter_scale * jnp.dot(
        projected_values, adapter_up_weight[1], preferred_element_type=jnp.float32
    )
    readout_rows = readout.reshape(token_count, key_value_columns)
    tok_ref = jnp.sum(readout_rows * reference_keys * reference_values, axis=1).reshape(
        pair_count, two_seqs, positions
    )
    tok_pol = jnp.sum(readout_rows * policy_keys * policy_values, axis=1).reshape(
        pair_count, two_seqs, positions
    )
    local_pos = jnp.arange(positions, dtype=jnp.int32)
    response_mask = (local_pos[None, None, :] >= (positions - response_length)[:, :, None]).astype(
        jnp.float32
    )
    seq_ref = jnp.sum(response_mask * tok_ref, axis=2)
    seq_pol = jnp.sum(response_mask * tok_pol, axis=2)
    pair_sign = jnp.where(
        jnp.arange(2, dtype=jnp.int32)[None, :] == chosen[:, None], 1.0, -1.0
    ).astype(jnp.float32)
    margin = jnp.sum(pair_sign * (seq_pol - seq_ref), axis=1)
    pair_weight = -preference_beta * jax.nn.sigmoid(-preference_beta * margin)
    coeff = (pair_weight[:, None, None] * pair_sign[:, :, None] * response_mask).reshape(
        token_count, 1
    )
    key_gradient = (coeff * readout_rows * policy_values).astype(jnp.bfloat16)
    value_gradient = (coeff * readout_rows * policy_keys).astype(jnp.bfloat16)
    contract_rows = (((0,), (0,)), ((), ()))
    up_local = jnp.stack(
        [
            adapter_scale
            * lax.dot_general(
                projected_keys, key_gradient, contract_rows, preferred_element_type=jnp.float32
            ),
            adapter_scale
            * lax.dot_general(
                projected_values, value_gradient, contract_rows, preferred_element_type=jnp.float32
            ),
        ]
    )
    back = jnp.concatenate(
        [
            adapter_scale
            * jnp.dot(key_gradient, adapter_up_weight[0].T, preferred_element_type=jnp.float32),
            adapter_scale
            * jnp.dot(value_gradient, adapter_up_weight[1].T, preferred_element_type=jnp.float32),
        ],
        axis=1,
    ).astype(jnp.bfloat16)
    columns = token_row_block
    down_share = lax.psum_scatter(
        lax.dot_general(columns, back, contract_rows, preferred_element_type=jnp.float32),
        "fsdp",
        scatter_dimension=0,
        tiled=True,
    )
    grad_down = lax.psum(down_share, "dp")
    grad_up = lax.psum(up_local, ("dp", "fsdp"))
    return (grad_down, grad_up)


def solution(mesh):
    placed = (
        P(("dp", "fsdp"), None, None, None),
        P("fsdp", None),
        P("fsdp", None),
        P(),
        P(("dp", "fsdp"), None, None, None),
        P(("dp", "fsdp")),
        P(("dp", "fsdp"), None),
    )
    return jax.shard_map(
        local, mesh=mesh, in_specs=placed, out_specs=(P("fsdp", None), P()), check_vma=False
    )
```

profile of v0, /device:TPU:1, one launch (start us, length us, event | category | flops | bytes accessed | tf_op | source)
XLA Modules:
  0.0 861.0 jit_solution(13829016809088052441)
XLA Ops:
  7.2 0.0 all-gather.5.cloned.1.call-start
  7.2 0.7 all-gather.5.cloned.1.call-update
  7.9 0.0 all-gather.3.cloned.1.call-start
  7.9 0.7 all-gather.3.cloned.1.call-update
  8.6 0.0 reduce-scatter.2.cloned.1.call-start
  9.4 0.7 subtract_bitcast_fusion
  10.0 42.9 %all-gather.5.cloned.1.call-done = bf16[8192,128]{1,0:T(8,128)(2,1)} async-done(((bf16[1024,128]{1,0:T(8,128)(2,1)}), bf16[8192,128]{1,0:T(8,128)(2,1)}) %all-gather.5.cloned.1.call-update) | async-done | bytes 2097168 | tf_op jit(solution)/shard_map/all_gather | solution.py:26
  52.9 6.9 convolution_convert_fusion
  59.8 172.2 %all-gather.3.cloned.1.call-done = bf16[8192,1024]{1,0:T(8,128)(2,1)} async-done(((bf16[1024,1024]{1,0:T(8,128)(2,1)}), bf16[8192,1024]{1,0:T(8,128)(2,1)}) %all-gather.3.cloned.1.call-update) | async-done | bytes 16777232 | tf_op jit(solution)/shard_map/all_gather | solution.py:21
  232.0 14.3 %fusion.31 = f32[512,1024]{1,0:T(8,128)S(1)} fusion(bf16[512,8192]{1,0:T(8,128)(2,1)} %bitcast.45, bf16[8192,1024]{1,0:T(8,128)(2,1)} %all-gather.3.cloned.1.call-done), kind=kOutput, calls=%fused_computation.51 | convolution fusion | flops 8589934592 | bytes 27262976 | tf_op jit(solution)/shard_map/dot_general | solution.py:19
  246.3 0.3 fusion.1
  246.6 0.5 fusion.13
  247.2 0.2 select_reduce_fusion
  247.4 0.6 multiply_reduce_fusion
  248.7 0.1 mul.108
  248.8 0.1 ge.42
  248.9 1.3 fusion.8
  250.2 0.3 fusion.5
  250.4 0.3 fusion.4
  250.7 6.7 convolution_bitcast_fusion
  257.4 0.0 reduce-scatter.2.cloned.1.call-update
  257.4 0.0 all-reduce.3.cloned.1.call-start
  257.5 54.6 %reduce-scatter.2.cloned.1.call-done = f32[1024,128]{0,1:T(8,128)} async-done(((f32[8192,128]{0,1:T(8,128)}), f32[1024,128]{0,1:T(8,128)}) %reduce-scatter.2.cloned.1.call-update) | async-done | bytes 524304 | tf_op jit(solution)/shard_map/reduce_scatter | solution.py:86
  312.1 0.0 all-reduce.3.cloned.1.call-update
  312.1 0.0 all-reduce.5.cloned.1.call-start
  312.2 0.2 fusion.6
  312.4 0.2 fusion.7
  312.6 0.7 pad_maximum_fusion
  313.4 284.7 %all-reduce.3.cloned.1.call-done = f32[1024,128]{0,1:T(8,128)} async-done(((f32[1024,128]{0,1:T(8,128)}), f32[1024,128]{0,1:T(8,128)}) %all-reduce.3.cloned.1.call-update) | async-done | bytes 524304 | tf_op jit(solution)/shard_map/psum | solution.py:92
  598.1 2.0 copy.14
  600.1 252.7 %all-reduce.5.cloned.1.call-done = f32[2,64,512]{2,1,0:T(8,128)} async-done(((f32[2,64,512]{2,1,0:T(8,128)}), f32[2,64,512]{2,1,0:T(8,128)}) %all-reduce.5.cloned.1.call-update) | async-done | bytes 262160 | tf_op jit(solution)/shard_map/psum | solution.py:93
  852.8 1.7 copy.21
  (11 shorter events, 0.1 us)
Async XLA Ops:
  7.2 45.7 %all-gather.5.cloned.1.call-start = ((), (), s32[]{:S(2)}) async-start(), calls=%async_computation.2 | async-start | bytes 2359296 | tf_op jit(solution)/shard_map/all_gather | solution.py:26
  7.9 224.1 %all-gather.3.cloned.1.call-start = ((), (), s32[]{:S(2)}) async-start(), calls=%async_computation.1 | async-start | bytes 18874368 | tf_op jit(solution)/shard_map/all_gather | solution.py:21
  8.6 303.5 %reduce-scatter.2.cloned.1.call-start = ((), (), s32[]{:S(2)}) async-start(), calls=%async_computation.3 | async-start | bytes 4718592 | tf_op jit(solution)/shard_map/reduce_scatter | solution.py:86
  59.8 186.5 %copy-start.1 = (bf16[2,64,512]{2,1,0:T(8,128)(2,1)S(1)}, bf16[2,64,512]{2,1,0:T(8,128)(2,1)}, u32[]{:S(2)}) copy-start(bf16[2,64,512]{2,1,0:T(8,128)(2,1)} %param.10) | copy-start | bytes 393220
  59.8 186.8 %copy-start = (bf16[1,2,256,512]{3,2,1,0:T(8,128)(2,1)S(1)}, bf16[1,2,256,512]{3,2,1,0:T(8,128)(2,1)}, u32[]{:S(2)}) copy-start(bf16[1,2,256,512]{3,2,1,0:T(8,128)(2,1)} %param.11) | copy-start | bytes 1572868
  257.4 340.6 %all-reduce.3.cloned.1.call-start = ((), (), s32[]{:S(2)}) async-start(), calls=%async_computation.4 | async-start | bytes 1048576 | tf_op jit(solution)/shard_map/psum | solution.py:92
  312.1 540.7 %all-reduce.5.cloned.1.call-start = ((), (), s32[]{:S(2)}) async-start(), calls=%async_computation.5 | async-start | bytes 524288 | tf_op jit(solution)/shard_map/psum | solution.py:93
Sparse Core Ops, SparseCore 0:
  9.8 43.0 all-gather.4
  54.7 177.2 all-gather.2
  257.6 54.5 reduce-scatter.1
  314.6 283.4 all-reduce.2
  604.8 247.9 all-reduce.4
where the time goes:
time: 862 us; the launch traced here: 861 us
  waiting for transfers between devices  809 us (94%)
  matrix products  29.6 us (3%)
  between operations  15.3 us (2%)
    psum x1, waiting for transfers between devices, local(): grad_down = lax.psum(down_share, 'dp')  285 us
    psum x1, waiting for transfers between devices, local(): grad_up = lax.psum(up_local, ('dp', 'fsdp'))  253 us
    all_gather x1, waiting for transfers between devices, local(): lax.all_gather(frozen_weight, 'fsdp', axis=0, tiled=True)  172 us
    reduce_scatter x1, waiting for transfers between devices, local(): lax.psum_scatter(lax.dot_general(columns, back, contract_rows, preferred_...  54.6 us
    all_gather x1, waiting for transfers between devices, local(): lax.all_gather(adapter_down_weight, 'fsdp', axis=0, tiled=True)  42.9 us
  transfers between devices with their start and end apart: 5, of which 5 were waited for; matrix products, arithmetic and copies ran while one was open for 1% of the time, Pallas kernels for 0%

commit v1 on v0

v1 whole, which is shorter than its diff:
```python
import jax
import jax.numpy as jnp
from jax import lax
from jax.experimental import pallas as pl
from jax.experimental.pallas import tpu as pltpu
from jax.sharding import PartitionSpec as P

MESH = pl.DeviceIdType.MESH
F32 = jnp.float32
BF16 = jnp.bfloat16
adapter_scale = 0.5
preference_beta = 0.1

HALF = 512
COMMON = 96
SHARE = 80
WIDE = 1152


def kernel(
    hid, fw, ad, up_h, ro_h, chosen, lengths, od, ou,
    W, H, acc, R, up, ro, pol, low, gk, gv, BT, U, UT, US1, US2, UA, UB,
    D, RZ, E, D2, RY, S1, S2, G, GT,
    loc, hs, hr, ys, yr, zs, zr, xs, xr, ps, pr, ts, tr, us, ur, vs, vr, qs, qr, ws, wr, ss, sr, gs, gr,
):
    dp = lax.axis_index("dp")
    fs = lax.axis_index("fsdp")
    zh, x, c = dp // 8, (dp // 2) % 4, dp % 2
    zl, y = fs // 4, fs % 4
    me16 = dp // 2
    z = zh * 2 + zl

    def dev(zh_, x_, c_, zl_, y_):
        return ((zh_ * 4 + x_) * 2 + c_, zl_ * 4 + y_)

    def at_y(n):
        return dev(zh, x, c, zl, (y + n + 4) % 4)

    def at_z(n):
        zz = (z + n + 8) % 8
        return dev(zz // 2, x, c, zz % 2, y)

    twin = dev(zh, x, 1 - c, zl, y)
    pa, pb = x % 2, x // 2
    x_a = dev(zh, x + 1 - 2 * pa, c, zl, y)
    x_b = dev(zh, (x + 3 + 2 * pa) % 4, c, zl, y)
    y_to = (at_y(1), at_y(-1))
    z_to = (at_z(1), at_z(-1))
    x_to = (x_a, x_b)

    def peer16(k):
        j = (me16 + k) % 16
        return (j * 2 + c, fs)

    def peer8(k):
        return (dp, (fs + k) % 8)

    def rc(src, dst, s, r, d):
        return pltpu.make_async_remote_copy(
            src_ref=src, dst_ref=dst, send_sem=s, recv_sem=r, device_id=d, device_id_type=MESH
        )

    mine = fs
    w_in = [
        pltpu.make_async_copy(
            fw.at[pl.ds(pl.multiple_of(c * HALF, HALF), HALF), :],
            W.at[mine, :, pl.ds(0, 1024)], loc.at[0]),
        pltpu.make_async_copy(
            ad.at[pl.ds(pl.multiple_of(c * HALF, HALF), HALF), :],
            W.at[mine, :, pl.ds(1024, 128)], loc.at[1]),
    ]
    others_in = [
        pltpu.make_async_copy(ro_h.at[0], ro, loc.at[2]),
        pltpu.make_async_copy(up_h, up, loc.at[3]),
    ]

    def h_cols(p, core):
        return pl.ds(pl.multiple_of(p * 1024 + core * HALF, HALF), HALF)

    h_in = [
        pltpu.make_async_copy(hid.at[0, :, :, h_cols(p, c)], H.at[p, pl.ds(0, 2)], loc.at[4 + p])
        for p in range(8)
    ]
    for cp in w_in + h_in + others_in:
        cp.start()

    bar = pltpu.get_barrier_semaphore()
    z_other = at_z(2 * zl - 1)
    pl.semaphore_signal(bar, inc=1, device_id=twin, device_id_type=MESH)
    pl.semaphore_signal(bar, inc=1, device_id=z_other, device_id_type=MESH)
    for k in range(1, 8):
        pl.semaphore_signal(bar, inc=1, device_id=peer8(k), device_id_type=MESH)
    for k in range(1, 16):
        pl.semaphore_signal(bar, inc=1, device_id=peer16(k), device_id_type=MESH)
    pl.semaphore_wait(bar, 24)

    started = []

    def go(cp):
        cp.start()
        started.append(cp)

    h_out = [
        rc(hid.at[0, :, :, h_cols(p, 1 - c)], H.at[p, pl.ds(2, 2)], hs.at[p], hr.at[p], twin)
        for p in range(8)
    ]

    def piece(dz, dy):
        zz = zl if dz == 0 else 1 - zl
        return zz * 4 + (y + dy) % 4

    def rows_share(d, other=False):
        par = pa if d == 0 else pb
        if other:
            par = 1 - par
        base = 2 * COMMON + d * 2 * SHARE
        return pl.ds(pl.multiple_of(base + SHARE * par, 16), SHARE)

    def rows_common(d):
        return pl.ds(COMMON * d, COMMON)

    def y_msg(d, m, received):
        step = 1 - 2 * d
        back = 1 if m in (2, 4) else 0
        dy = -step * (back + (1 if received else 0))
        rows = {0: rows_share(d), 1: rows_common(d), 2: rows_share(d), 3: rows_share(1 - d),
                4: rows_common(d), 5: rows_common(1 - d)}[m]
        ref = W.at[piece(0, dy % 4), rows, :]
        return rc(ref, ref, ys.at[d, m], yr.at[d, m], y_to[d])

    def z_msg(d, dy, m, received):
        rows = rows_share(d) if m == 0 else rows_common(d)
        ref = W.at[piece(1 if received else 0, dy % 4), rows, :]
        return rc(ref, ref, zs.at[d, dy % 4, m], zr.at[d, dy % 4, m], z_to[d])

    def x_msg(d, dz, dy, received):
        ref = W.at[piece(dz, dy % 4), rows_share(d, received), :]
        i = dz * 4 + dy % 4
        return rc(ref, ref, xs.at[d, i], xr.at[d, i], x_to[d])

    def mm(p, first, blocks):
        @pl.loop(blocks[0], blocks[1])
        def _(tb):
            h = H[p, tb]
            for nb in range(3):
                cols = pl.ds(nb * 384, 384)
                r = jnp.dot(h, W[p, :, cols], preferred_element_type=F32)
                if first:
                    acc[tb, :, cols] = r
                else:
                    acc[tb, :, cols] += r

    for cp in w_in:
        cp.wait()
    for d in range(2):
        go(y_msg(d, 0, False))
        go(z_msg(d, 0, 0, False))
    for p in range(4):
        go(h_out[p])
    for d in range(2):
        go(y_msg(d, 1, False))
        go(z_msg(d, 0, 1, False))
    for p in range(4, 8):
        go(h_out[p])

    for d in range(2):
        s = 1 - 2 * d
        y_msg(d, 0, True).wait_recv()
        go(y_msg(d, 2, False))
        go(y_msg(d, 3, False))
        go(z_msg(d, -s, 0, False))
        go(x_msg(d, 0, -s, False))
    for d in range(2):
        z_msg(d, 0, 0, True).wait_recv()
        go(x_msg(d, 1, 0, False))
    for d in range(2):
        s = 1 - 2 * d
        y_msg(d, 1, True).wait_recv()
        go(y_msg(d, 4, False))
        go(y_msg(d, 5, False))
        go(z_msg(d, -s, 1, False))
    for cp in h_in:
        cp.wait()
    for cp in h_out:
        cp.wait_recv()
    mm(piece(0, 0), True, (0, 4))
    for d in range(2):
        s = 1 - 2 * d
        y_msg(d, 2, True).wait_recv()
        go(z_msg(d, 2, 0, False))
        go(x_msg(d, 0, 2, False))
        z_msg(d, -s, 0, True).wait_recv()
        go(x_msg(d, 1, -s, False))
    for d in range(2):
        z_msg(d, 0, 1, True).wait_recv()
        x_msg(d, 1, 0, True).wait_recv()
    mm(piece(1, 0), False, (0, 4))
    for d in range(2):
        s = 1 - 2 * d
        y_msg(1 - d, 3, True).wait_recv()
        go(z_msg(d, s, 0, False))
        go(x_msg(d, 0, s, False))
    for d in range(2):
        y_msg(d, 4, True).wait_recv()
        go(z_msg(d, 2, 1, False))
        z_msg(d, 2, 0, True).wait_recv()
        go(x_msg(d, 1, 2, False))
    for d in range(2):
        s = 1 - 2 * d
        y_msg(1 - d, 5, True).wait_recv()
        go(z_msg(d, s, 1, False))
        z_msg(d, s, 0, True).wait_recv()
        go(x_msg(d, 1, s, False))
    for dy in (2, 1, 3):
        for d in range(2):
            x_msg(d, 0, dy, True).wait_recv()
        mm(piece(0, dy), False, (0, 4))
    for d in range(2):
        z_msg(d, 2, 1, True).wait_recv()
        x_msg(d, 1, 2, True).wait_recv()
    mm(piece(1, 2), False, (0, 4))
    for dy in (1, 3):
        for d in range(2):
            z_msg(d, dy, 1, True).wait_recv()
            x_msg(d, 1, dy, True).wait_recv()
        mm(piece(1, dy), False, (2, 4))
    part = [rc(acc.at[2 + s], R.at[s], ps.at[s], pr.at[s], twin) for s in range(2)]
    for cp in part:
        go(cp)
    for dy in (1, 3):
        mm(piece(1, dy), False, (0, 2))
    for cp in others_in:
        cp.wait()
    for cp in part:
        cp.wait_recv()

    for s in range(2):
        t = (acc[s, :, pl.ds(1024, 128)] + R[s, :, pl.ds(1024, 128)]).astype(BF16)
        low[pl.ds(s * 256, 256), :] = t
        for i in range(2):
            pol[s, :, pl.ds(i * 512, 512)] = adapter_scale * jnp.dot(
                t[:, i * 64:(i + 1) * 64], up[i], preferred_element_type=F32)

    def token_weight(s, r):
        pos = r * 32 + lax.broadcasted_iota(jnp.int32, (32, 1), 0)
        sign = jnp.where(chosen[0] == s, 1.0, -1.0).astype(F32)
        return jnp.where(pos >= 256 - lengths[0, s], sign, 0.0)

    total = jnp.zeros((32, 512), F32)
    for s in range(2):
        def first_pass(r, total, s=s):
            rows = pl.ds(pl.multiple_of(r * 32, 32), 32)
            kr = acc[s, rows, pl.ds(0, 512)] + R[s, rows, pl.ds(0, 512)]
            vr = acc[s, rows, pl.ds(512, 512)] + R[s, rows, pl.ds(512, 512)]
            kp = kr + pol[s, rows, pl.ds(0, 512)]
            vp = vr + pol[s, rows, pl.ds(512, 512)]
            pol[s, rows, pl.ds(0, 512)] = kp
            pol[s, rows, pl.ds(512, 512)] = vp
            read = ro[s, rows, :].astype(F32)
            return total + token_weight(s, r) * (read * (kp * vp - kr * vr))
        total = lax.fori_loop(0, 8, first_pass, total)
    margin = jnp.sum(jnp.sum(total, axis=0, keepdims=True), axis=1, keepdims=True)
    pair_weight = -preference_beta * jax.nn.sigmoid(-preference_beta * margin)

    for s in range(2):
        def second_pass(r, carry, s=s):
            rows = pl.ds(pl.multiple_of(r * 32, 32), 32)
            whole = pl.ds(pl.multiple_of(s * 256 + r * 32, 32), 32)
            read = (pair_weight * token_weight(s, r)) * ro[s, rows, :].astype(F32)
            gk[whole, :] = (read * pol[s, rows, pl.ds(512, 512)]).astype(BF16)
            gv[whole, :] = (read * pol[s, rows, pl.ds(0, 512)]).astype(BF16)
            return carry
        lax.fori_loop(0, 8, second_pass, 0)

    nt = (((1,), (1,)), ((), ()))
    for i, g in enumerate((gk, gv)):
        BT[0, pl.ds(i * 64, 64), :] = (adapter_scale * lax.dot_general(
            up[i], g[...], nt, preferred_element_type=F32)).astype(BF16)
    b_cp = rc(BT.at[0], BT.at[1], ts.at[0], tr.at[0], twin)
    go(b_cp)
    low_t = jnp.transpose(low[...].astype(F32)).astype(BF16)
    for i, g in enumerate((gk, gv)):
        U[i] = adapter_scale * jnp.dot(
            low_t[i * 64:(i + 1) * 64, :], g[...], preferred_element_type=F32)
    u_cp = rc(U.at[1 - c], UT, ts.at[1], tr.at[1], twin)
    go(u_cp)
    b_cp.wait_recv()

    def grad(p):
        own = jnp.dot(BT[0], H[p, pl.ds(0, 2)].reshape(512, 512), preferred_element_type=F32)
        return own + jnp.dot(BT[1], H[p, pl.ds(2, 2)].reshape(512, 512), preferred_element_type=F32)

    zd = []
    for dy in (2, 1, 3, 0):
        D[dy] = grad(piece(1, dy)).astype(BF16)
        for d in range(2):
            h = pl.ds(d * 64, 64)
            cp = rc(D.at[dy, h], RZ.at[dy, h], us.at[dy, d], ur.at[dy, d], z_to[d])
            go(cp)
            zd.append((dy, cp))

    u_cp.wait_recv()
    chip = U[c] + UT[...]
    for j in range(16):
        r, q = j // 4, j % 4
        US1[j] = chip[r * 16:(r + 1) * 16, q * 128:(q + 1) * 128].astype(BF16)

    def spread16(src, dst, send, recv):
        def one(k, carry):
            j = (me16 + k) % 16
            rc(src(j), dst.at[me16], send.at[k], recv.at[k], peer16(k)).start()
            return carry
        lax.fori_loop(1, 16, one, 0)

    def land16(src, dst, send, recv):
        def one(k, carry):
            j = (me16 + 16 - k) % 16
            rc(src(j), dst.at[j], send.at[k], recv.at[k], peer16(k)).wait_recv()
            return carry
        lax.fori_loop(1, 16, one, 0)

    def sent16(src, dst, send, recv):
        def one(k, carry):
            j = (me16 + k) % 16
            rc(src(j), dst.at[me16], send.at[k], recv.at[k], peer16(k)).wait_send()
            return carry
        lax.fori_loop(1, 16, one, 0)

    u_args = (lambda j: US1.at[j], US2, vs, vr)
    spread16(*u_args)
    US2[me16] = US1[me16]

    for dy in (2, 1, 3, 0):
        E[dy] = grad(piece(0, dy))
    yd = []
    for dy in (2, 1, 3, 0):
        for dd, cp in zd:
            if dd == dy:
                cp.wait_recv()
        t = E[dy] + RZ[dy].astype(F32)
        if dy:
            D2[dy] = t.astype(BF16)
            cp = rc(D2.at[dy], RY.at[dy], qs.at[dy], qr.at[dy], at_y(dy))
            go(cp)
            yd.append(cp)
        else:
            E[0] = t

    land16(*u_args)
    UA[...] = jnp.sum(US2[...].astype(F32), axis=0).astype(BF16)
    UB[fs] = UA[...]
    for k in range(1, 8):
        go(rc(UA, UB.at[fs], ws.at[k], wr.at[k], peer8(k)))

    for cp in yd:
        cp.wait_recv()
    t = E[0] + RY[1].astype(F32) + RY[2].astype(F32) + RY[3].astype(F32)
    S1[...] = jnp.transpose(t).astype(BF16).reshape(16, 32, 128)
    s_args = (lambda j: S1.at[j], S2, ss, sr)
    spread16(*s_args)
    S2[me16] = S1[me16]
    for k in range(1, 8):
        rc(UA, UB.at[(fs + 8 - k) % 8], ws.at[k], wr.at[k], peer8(k)).wait_recv()
    G[me16, pl.ds(32, 16), :] = jnp.sum(UB[...].astype(F32), axis=0).astype(BF16)
    land16(*s_args)
    G[me16, pl.ds(0, 32), :] = jnp.sum(S2[...].astype(F32), axis=0).astype(BF16)
    g_args = (lambda j: G.at[me16], G, gs, gr)
    spread16(*g_args)

    def land_g(k, carry):
        j = (me16 + 16 - k) % 16
        rc(G.at[j], G.at[j], gs.at[k], gr.at[k], peer16(k)).wait_recv()
        return carry
    lax.fori_loop(1, 16, land_g, 0)
    t_cp = rc(G, GT, ts.at[2], tr.at[2], twin)
    go(t_cp)

    def place(src, core):
        for j in range(16):
            od[pl.ds(pl.multiple_of(core * 512 + j * 32, 32), 32), :] = src[j, pl.ds(0, 32), :].astype(F32)
            ou[core, pl.ds((j // 4) * 16, 16), pl.ds((j % 4) * 128, 128)] = src[j, pl.ds(32, 16), :].astype(F32)

    place(G, c)
    t_cp.wait_recv()
    place(GT, 1 - c)

    for cp in started:
        cp.wait_send()
    sent16(*u_args)
    sent16(*s_args)
    sent16(*g_args)


def local(hidden, frozen_weight, adapter_down_weight, adapter_up_weight, readout, chosen, response_length):
    dma = pltpu.SemaphoreType.DMA
    vmem = pltpu.VMEM
    anywhere = pl.BlockSpec(memory_space=pl.ANY)
    smem = pl.BlockSpec(memory_space=pltpu.SMEM)
    return pl.pallas_call(
        kernel,
        out_shape=(
            jax.ShapeDtypeStruct((1024, 128), F32),
            jax.ShapeDtypeStruct((2, 64, 512), F32),
        ),
        in_specs=[anywhere] * 5 + [smem] * 2,
        out_specs=(pl.BlockSpec(memory_space=pltpu.VMEM), pl.BlockSpec(memory_space=pltpu.VMEM)),
        scratch_shapes=[
            vmem((8, HALF, WIDE), BF16),
            vmem((8, 4, 256, HALF), BF16),
            vmem((4, 256, WIDE), F32),
            vmem((2, 256, WIDE), F32),
            vmem((2, 64, 512), BF16),
            vmem((2, 256, 512), BF16),
            vmem((2, 256, 1024), F32),
            vmem((512, 128), BF16),
            vmem((512, 512), BF16),
            vmem((512, 512), BF16),
            vmem((2, 128, 512), BF16),
            vmem((2, 64, 512), F32),
            vmem((64, 512), F32),
            vmem((16, 16, 128), BF16),
            vmem((16, 16, 128), BF16),
            vmem((16, 128), BF16),
            vmem((8, 16, 128), BF16),
            vmem((4, 128, 512), BF16),
            vmem((4, 128, 512), BF16),
            vmem((4, 128, 512), F32),
            vmem((4, 128, 512), BF16),
            vmem((4, 128, 512), BF16),
            vmem((16, 32, 128), BF16),
            vmem((16, 32, 128), BF16),
            vmem((16, 48, 128), BF16),
            vmem((16, 48, 128), BF16),
            dma((12,)),
            dma((8,)), dma((8,)),
            dma((2, 6)), dma((2, 6)),
            dma((2, 4, 2)), dma((2, 4, 2)),
            dma((2, 8)), dma((2, 8)),
            dma((2,)), dma((2,)),
            dma((3,)), dma((3,)),
            dma((4, 2)), dma((4, 2)),
            dma((16,)), dma((16,)),
            dma((4,)), dma((4,)),
            dma((8,)), dma((8,)),
            dma((16,)), dma((16,)),
            dma((16,)), dma((16,)),
        ],
        compiler_params=pltpu.CompilerParams(
            collective_id=0, has_side_effects=True, vmem_limit_bytes=56 * 2**20
        ),
        cost_estimate=pl.CostEstimate(flops=12 * 10**9, bytes_accessed=12 * 10**6, transcendentals=1),
    )(hidden, frozen_weight, adapter_down_weight, adapter_up_weight, readout, chosen, response_length)


def solution(mesh):
    placed = (
        P(("dp", "fsdp"), None, None, None),
        P("fsdp", None),
        P("fsdp", None),
        P(),
        P(("dp", "fsdp"), None, None, None),
        P(("dp", "fsdp")),
        P(("dp", "fsdp"), None),
    )
    return jax.shard_map(
        local, mesh=mesh, in_specs=placed, out_specs=(P("fsdp", None), P()), check_vma=False
    )
```

time: 862 us -> 95.2 us (0.11)
  waiting for transfers between devices: 809 us -> 0 us
  Pallas kernels: 0 us -> 90.2 us
  matrix products: 29.6 us -> 0 us
  between operations: 15.3 us -> 1.29 us
    psum x2 -> x0, waiting for transfers between devices: 537 us -> none  [the longest x1 285 us: local(): grad_down = lax.psum(down_share, 'dp')]
    all_gather x2 -> x0, waiting for transfers between devices: 215 us -> none  [the longest x1 172 us: local(): lax.all_gather(frozen_weight, 'fsdp', axis=0, tiled=True)]
    pallas_call x0 -> x1, Pallas kernels: none -> 90.2 us  [local(): pl.pallas_call(kernel, out_shape=(jax.ShapeDtypeStruct((1024, 128), F32),...]
    reduce_scatter x1 -> x0, waiting for transfers between devices: 54.6 us -> none  [local(): lax.psum_scatter(lax.dot_general(columns, back, contract_rows, preferred_...]
    dot_general x9 -> x0, matrix products: 29.6 us -> none  [the longest x1 14.3 us: local(): jnp.dot(columns, lax.all_gather(frozen_weight, 'fsdp', axis=0, tiled=True...]
  transfers between devices with their start and end apart: 5 -> 0, of which waited for: 5 -> 0; matrix products, arithmetic and copies ran while one was open for 1% -> 0% of each run, Pallas kernels for 0% -> 0%
where the time goes in v1:
time: 95.2 us; the launch traced here: 95 us
  Pallas kernels  90.2 us (95%)
  local copies, waits for them, and re-layouts  3.54 us (4%)
  between operations  1.29 us (1%)
    pallas_call x1, Pallas kernels, local(): pl.pallas_call(kernel, out_shape=(jax.ShapeDtypeStruct((1024, 128), F32),...  90.2 us
    unnamed x2, local copies, waits for them, and re-layouts  3.54 us

profile of v1, /device:TPU:1, one launch (start us, length us, event | category | flops | bytes accessed | tf_op | source)
XLA Modules:
  0.0 95.0 jit_solution(7755168789679194899)
XLA Ops:
  1.3 90.2 %shard_map.86 = (f32[1024,128]{1,0:T(8,128)}, f32[2,64,512]{2,1,0:T(8,128)}) custom-call(bf16[1,2,256,8192]{3,2,1,0:T(8,128)(2,1)} %hid.1, bf16[1024,1024]{1,0:T(8,128)(2,1)} %fw.1, bf16[1024,128]{1,0:T(8,128)(2,1)} %ad.1, bf16[2,64,512]{2,1,0:T(8,128)(2,1)} %up_h.1, bf16[1,2,256,512]{3,2,1,0:T(8,128)(2,1)} %ro_h.1, s32[1]{0:T(128)S(6)} %copy.11.chosen, ...), custom_call_target="tpu_custom_call" | custom-call | flops 12000000000 | bytes 12000000 | tf_op jit(solution)/shard_map/pallas_call | solution.py:399
  91.5 1.9 %copy.12 = f32[1024,128]{1,0:T(8,128)} copy(f32[1024,128]{1,0:T(8,128)} %get-tuple-element.4) | data formatting | bytes 1048576
  93.3 1.7 %copy.13 = f32[2,64,512]{2,1,0:T(8,128)} copy(f32[2,64,512]{2,1,0:T(8,128)} %get-tuple-element.5) | data formatting | bytes 524288

commit v2 on v1

--- a/solution.py
+++ b/solution.py
@@ -18,10 +18,10 @@
 
 
 def kernel(
-    hid, fw, ad, up_h, ro_h, chosen, lengths, od, ou,
-    W, H, acc, R, up, ro, pol, low, gk, gv, BT, U, UT, US1, US2, UA, UB,
-    D, RZ, E, D2, RY, S1, S2, G, GT,
-    loc, hs, hr, ys, yr, zs, zr, xs, xr, ps, pr, ts, tr, us, ur, vs, vr, qs, qr, ws, wr, ss, sr, gs, gr,
+    hid, fw, ad, up_h, ro_h, chosen, lengths, GD, GU,
+    W, H, acc, R, L, RL, up, ro, pol, low, gk, gv, BT, U, UT, US1, US2, UA, UB,
+    D, RZ, E, D2, RY, S1, S2,
+    loc, hs, hr, ys, yr, zs, zr, xs, xr, ps, pr, ts, tr, us, ur, vs, vr, qs, qr, ws, wr, ss, sr, gs, gr, es, er,
 ):
     dp = lax.axis_index("dp")
     fs = lax.axis_index("fsdp")
@@ -138,17 +138,32 @@
         i = dz * 4 + dy % 4
         return rc(ref, ref, xs.at[d, i], xr.at[d, i], x_to[d])
 
-    def mm(p, first, blocks):
-        @pl.loop(blocks[0], blocks[1])
-        def _(tb):
-            h = H[p, tb]
-            for nb in range(3):
-                cols = pl.ds(nb * 384, 384)
-                r = jnp.dot(h, W[p, :, cols], preferred_element_type=F32)
+    def tokens(p, half):
+        return H[p, pl.ds(half * 2, 2)].reshape(512, HALF)
+
+    def mm(p, first, halves):
+        for half in halves:
+            for lo, n in ((0, 512), (512, 512), (1024, 128)):
+                cols = pl.ds(lo, n)
+                r = jnp.dot(tokens(p, half), W[p, :, cols], preferred_element_type=F32).reshape(2, 256, n)
                 if first:
-                    acc[tb, :, cols] = r
+                    acc[pl.ds(half * 2, 2), :, cols] = r
                 else:
-                    acc[tb, :, cols] += r
+                    acc[pl.ds(half * 2, 2), :, cols] += r
+
+    def mm_last(half):
+        p, q = piece(1, 1), piece(1, 3)
+
+        @pl.loop(0, 3)
+        def _(nb):
+            cols = pl.ds(pl.multiple_of(nb * 384, 384), 384)
+            r = jnp.dot(tokens(p, half), W[p, :, cols], preferred_element_type=F32)
+            r += jnp.dot(tokens(q, half), W[q, :, cols], preferred_element_type=F32)
+            r = r.reshape(2, 256, 384)
+            if half:
+                L[:, :, cols] = r.astype(BF16)
+            else:
+                acc[pl.ds(0, 2), :, cols] += r
 
     for cp in w_in:
         cp.wait()
@@ -183,7 +198,7 @@
         cp.wait()
     for cp in h_out:
         cp.wait_recv()
-    mm(piece(0, 0), True, (0, 4))
+    mm(piece(0, 0), True, (0, 1))
     for d in range(2):
         s = 1 - 2 * d
         y_msg(d, 2, True).wait_recv()
@@ -194,7 +209,7 @@
     for d in range(2):
         z_msg(d, 0, 1, True).wait_recv()
         x_msg(d, 1, 0, True).wait_recv()
-    mm(piece(1, 0), False, (0, 4))
+    mm(piece(1, 0), False, (0, 1))
     for d in range(2):
         s = 1 - 2 * d
         y_msg(1 - d, 3, True).wait_recv()
@@ -214,28 +229,30 @@
     for dy in (2, 1, 3):
         for d in range(2):
             x_msg(d, 0, dy, True).wait_recv()
-        mm(piece(0, dy), False, (0, 4))
+        mm(piece(0, dy), False, (0, 1))
     for d in range(2):
         z_msg(d, 2, 1, True).wait_recv()
         x_msg(d, 1, 2, True).wait_recv()
-    mm(piece(1, 2), False, (0, 4))
+    mm(piece(1, 2), False, (1,))
+    early = rc(acc.at[pl.ds(2, 2)], R, ps.at[0], pr.at[0], twin)
+    go(early)
+    mm(piece(1, 2), False, (0,))
     for dy in (1, 3):
         for d in range(2):
             z_msg(d, dy, 1, True).wait_recv()
             x_msg(d, 1, dy, True).wait_recv()
-        mm(piece(1, dy), False, (2, 4))
-    part = [rc(acc.at[2 + s], R.at[s], ps.at[s], pr.at[s], twin) for s in range(2)]
-    for cp in part:
-        go(cp)
-    for dy in (1, 3):
-        mm(piece(1, dy), False, (0, 2))
+    mm_last(1)
+    late = rc(L, RL, ps.at[1], pr.at[1], twin)
+    go(late)
+    mm_last(0)
     for cp in others_in:
         cp.wait()
-    for cp in part:
-        cp.wait_recv()
+    early.wait_recv()
+    late.wait_recv()
 
     for s in range(2):
-        t = (acc[s, :, pl.ds(1024, 128)] + R[s, :, pl.ds(1024, 128)]).astype(BF16)
+        t = (acc[s, :, pl.ds(1024, 128)] + R[s, :, pl.ds(1024, 128)]
+             + RL[s, :, pl.ds(1024, 128)].astype(F32)).astype(BF16)
         low[pl.ds(s * 256, 256), :] = t
         for i in range(2):
             pol[s, :, pl.ds(i * 512, 512)] = adapter_scale * jnp.dot(
@@ -250,8 +267,10 @@
     for s in range(2):
         def first_pass(r, total, s=s):
             rows = pl.ds(pl.multiple_of(r * 32, 32), 32)
-            kr = acc[s, rows, pl.ds(0, 512)] + R[s, rows, pl.ds(0, 512)]
-            vr = acc[s, rows, pl.ds(512, 512)] + R[s, rows, pl.ds(512, 512)]
+            kr = acc[s, rows, pl.ds(0, 512)] + (
+                R[s, rows, pl.ds(0, 512)] + RL[s, rows, pl.ds(0, 512)].astype(F32))
+            vr = acc[s, rows, pl.ds(512, 512)] + (
+                R[s, rows, pl.ds(512, 512)] + RL[s, rows, pl.ds(512, 512)].astype(F32))
             kp = kr + pol[s, rows, pl.ds(0, 512)]
             vp = vr + pol[s, rows, pl.ds(512, 512)]
             pol[s, rows, pl.ds(0, 512)] = kp
@@ -361,34 +380,31 @@
     S2[me16] = S1[me16]
     for k in range(1, 8):
         rc(UA, UB.at[(fs + 8 - k) % 8], ws.at[k], wr.at[k], peer8(k)).wait_recv()
-    G[me16, pl.ds(32, 16), :] = jnp.sum(UB[...].astype(F32), axis=0).astype(BF16)
+    GU[c, me16] = jnp.sum(UB[...].astype(F32), axis=0).astype(BF16)
+    gu_args = (lambda j: GU.at[c, me16], GU.at[c], es, er)
+    spread16(*gu_args)
     land16(*s_args)
-    G[me16, pl.ds(0, 32), :] = jnp.sum(S2[...].astype(F32), axis=0).astype(BF16)
-    g_args = (lambda j: G.at[me16], G, gs, gr)
-    spread16(*g_args)
-
-    def land_g(k, carry):
-        j = (me16 + 16 - k) % 16
-        rc(G.at[j], G.at[j], gs.at[k], gr.at[k], peer16(k)).wait_recv()
-        return carry
-    lax.fori_loop(1, 16, land_g, 0)
-    t_cp = rc(G, GT, ts.at[2], tr.at[2], twin)
-    go(t_cp)
-
-    def place(src, core):
-        for j in range(16):
-            od[pl.ds(pl.multiple_of(core * 512 + j * 32, 32), 32), :] = src[j, pl.ds(0, 32), :].astype(F32)
-            ou[core, pl.ds((j // 4) * 16, 16), pl.ds((j % 4) * 128, 128)] = src[j, pl.ds(32, 16), :].astype(F32)
-
-    place(G, c)
-    t_cp.wait_recv()
-    place(GT, 1 - c)
-
+    GD[c, me16] = jnp.sum(S2[...].astype(F32), axis=0).astype(BF16)
+    gd_args = (lambda j: GD.at[c, me16], GD.at[c], gs, gr)
+    spread16(*gd_args)
+    land16(*gu_args)
+    land16(*gd_args)
+    out = [rc(GD.at[c], GD.at[c], ts.at[2], tr.at[2], twin), rc(GU.at[c], GU.at[c], ts.at[3], tr.at[3], twin)]
+    for cp in out:
+        go(cp)
+    for cp in out:
+        cp.wait_recv()
     for cp in started:
         cp.wait_send()
-    sent16(*u_args)
-    sent16(*s_args)
-    sent16(*g_args)
+    for args in (u_args, s_args, gu_args, gd_args):
+        sent16(*args)
+
+
+def widen(gd, gu, od, ou):
+    od[...] = gd[...].astype(F32).reshape(1024, 128)
+    for core in range(2):
+        for j in range(16):
+            ou[core, pl.ds((j // 4) * 16, 16), pl.ds((j % 4) * 128, 128)] = gu[core, j].astype(F32)
 
 
 def local(hidden, frozen_weight, adapter_down_weight, adapter_up_weight, readout, chosen, response_length):
@@ -396,11 +412,11 @@
     vmem = pltpu.VMEM
     anywhere = pl.BlockSpec(memory_space=pl.ANY)
     smem = pl.BlockSpec(memory_space=pltpu.SMEM)
-    return pl.pallas_call(
+    gd, gu = pl.pallas_call(
         kernel,
         out_shape=(
-            jax.ShapeDtypeStruct((1024, 128), F32),
-            jax.ShapeDtypeStruct((2, 64, 512), F32),
+            jax.ShapeDtypeStruct((2, 16, 32, 128), BF16),
+            jax.ShapeDtypeStruct((2, 16, 16, 128), BF16),
         ),
         in_specs=[anywhere] * 5 + [smem] * 2,
         out_specs=(pl.BlockSpec(memory_space=pltpu.VMEM), pl.BlockSpec(memory_space=pltpu.VMEM)),
@@ -409,6 +425,8 @@
             vmem((8, 4, 256, HALF), BF16),
             vmem((4, 256, WIDE), F32),
             vmem((2, 256, WIDE), F32),
+            vmem((2, 256, WIDE), BF16),
+            vmem((2, 256, WIDE), BF16),
             vmem((2, 64, 512), BF16),
             vmem((2, 256, 512), BF16),
             vmem((2, 256, 1024), F32),
@@ -429,19 +447,18 @@
             vmem((4, 128, 512), BF16),
             vmem((16, 32, 128), BF16),
             vmem((16, 32, 128), BF16),
-            vmem((16, 48, 128), BF16),
-            vmem((16, 48, 128), BF16),
             dma((12,)),
             dma((8,)), dma((8,)),
             dma((2, 6)), dma((2, 6)),
             dma((2, 4, 2)), dma((2, 4, 2)),
             dma((2, 8)), dma((2, 8)),
             dma((2,)), dma((2,)),
-            dma((3,)), dma((3,)),
+            dma((4,)), dma((4,)),
             dma((4, 2)), dma((4, 2)),
             dma((16,)), dma((16,)),
             dma((4,)), dma((4,)),
             dma((8,)), dma((8,)),
+            dma((16,)), dma((16,)),
             dma((16,)), dma((16,)),
             dma((16,)), dma((16,)),
         ],
@@ -450,6 +467,16 @@
         ),
         cost_estimate=pl.CostEstimate(flops=12 * 10**9, bytes_accessed=12 * 10**6, transcendentals=1),
     )(hidden, frozen_weight, adapter_down_weight, adapter_up_weight, readout, chosen, response_length)
+    return pl.pallas_call(
+        widen,
+        out_shape=(
+            jax.ShapeDtypeStruct((1024, 128), F32),
+            jax.ShapeDtypeStruct((2, 64, 512), F32),
+        ),
+        in_specs=[pl.BlockSpec(memory_space=pltpu.VMEM)] * 2,
+        out_specs=(pl.BlockSpec(memory_space=pltpu.VMEM),) * 2,
+        cost_estimate=pl.CostEstimate(flops=10**6, bytes_accessed=2 * 10**6, transcendentals=0),
+    )(gd, gu)
 
 
 def solution(mesh):

time: 95.2 us -> 91.7 us (0.963)
  local copies, waits for them, and re-layouts: 3.54 us -> 0 us
    unnamed x2 -> x0, local copies, waits for them, and re-layouts: 3.54 us -> none
    pallas_call x1 -> x2, Pallas kernels: 90.2 us -> 90.3 us  [the longest x1 88.4 us: local(): pl.pallas_call(kernel, out_shape=(jax.ShapeDtypeStruct((2, 16, 32, 128),...]
where the time goes in v2:
time: 91.7 us; the launch traced here: 91.6 us
  Pallas kernels  90.3 us (98%)
  between operations  1.29 us (1%)
    pallas_call x1, Pallas kernels, local(): pl.pallas_call(kernel, out_shape=(jax.ShapeDtypeStruct((2, 16, 32, 128),...  88.4 us
    pallas_call x1, Pallas kernels, local(): pl.pallas_call(widen, out_shape=(jax.ShapeDtypeStruct((1024, 128), F32),...  1.9 us

profile of v2, /device:TPU:1, one launch (start us, length us, event | category | flops | bytes accessed | tf_op | source)
XLA Modules:
  0.0 91.6 jit_solution(17801588419727970507)
XLA Ops:
  1.3 88.4 %shard_map.86 = (bf16[2,16,32,128]{3,2,1,0:T(8,128)(2,1)}, bf16[2,16,16,128]{3,2,1,0:T(8,128)(2,1)}) custom-call(bf16[1,2,256,8192]{3,2,1,0:T(8,128)(2,1)} %hid.1, bf16[1024,1024]{1,0:T(8,128)(2,1)} %fw.1, bf16[1024,128]{1,0:T(8,128)(2,1)} %ad.1, bf16[2,64,512]{2,1,0:T(8,128)(2,1)} %up_h.1, bf16[1,2,256,512]{3,2,1,0:T(8,128)(2,1)} %ro_h.1, ...), custom_call_target="tpu_custom_call" | custom-call | flops 12000000000 | bytes 12000000 | tf_op jit(solution)/shard_map/pallas_call | solution.py:415
  89.7 1.9 %shard_map.87 = (f32[1024,128]{1,0:T(8,128)}, f32[2,64,512]{2,1,0:T(8,128)}) custom-call(bf16[2,16,32,128]{3,2,1,0:T(8,128)(2,1)} %get-tuple-element.4.gd, bf16[2,16,16,128]{3,2,1,0:T(8,128)(2,1)} %get-tuple-element.5.gu), custom_call_target="tpu_custom_call" | custom-call | flops 1000000 | bytes 2000000 | tf_op jit(solution)/shard_map/pallas_call | solution.py:470

commit v3 on v2

--- a/solution.py
+++ b/solution.py
@@ -21,7 +21,7 @@
     hid, fw, ad, up_h, ro_h, chosen, lengths, GD, GU,
     W, H, acc, R, L, RL, up, ro, pol, low, gk, gv, BT, U, UT, US1, US2, UA, UB,
     D, RZ, E, D2, RY, S1, S2,
-    loc, hs, hr, ys, yr, zs, zr, xs, xr, ps, pr, ts, tr, us, ur, vs, vr, qs, qr, ws, wr, ss, sr, gs, gr, es, er,
+    loc, hs, hr, ys, yr, zs, zr, xs, xr, ps, pr, ts, tr, us, ur, vs, vr, qs, qr, ws, wr, ss, sr, gs, gr, es, er, far,
 ):
     dp = lax.axis_index("dp")
     fs = lax.axis_index("fsdp")
@@ -85,14 +85,17 @@
         cp.start()
 
     bar = pltpu.get_barrier_semaphore()
-    z_other = at_z(2 * zl - 1)
-    pl.semaphore_signal(bar, inc=1, device_id=twin, device_id_type=MESH)
-    pl.semaphore_signal(bar, inc=1, device_id=z_other, device_id_type=MESH)
-    for k in range(1, 8):
-        pl.semaphore_signal(bar, inc=1, device_id=peer8(k), device_id_type=MESH)
-    for k in range(1, 16):
-        pl.semaphore_signal(bar, inc=1, device_id=peer16(k), device_id_type=MESH)
-    pl.semaphore_wait(bar, 24)
+    near = (twin,) + y_to + z_to + x_to
+    for d in near:
+        pl.semaphore_signal(bar, inc=1, device_id=d, device_id_type=MESH)
+    pl.semaphore_wait(bar, len(near))
+
+    def tell(i, to):
+        for d in to:
+            pl.semaphore_signal(far.at[i], inc=1, device_id=d, device_id_type=MESH)
+
+    def told(i):
+        pl.semaphore_wait(far.at[i], 2)
 
     started = []
 
@@ -178,6 +181,8 @@
     for p in range(4, 8):
         go(h_out[p])
 
+    tell(0, x_to)
+    tell(1, y_to)
     for d in range(2):
         s = 1 - 2 * d
         y_msg(d, 0, True).wait_recv()
@@ -188,12 +193,17 @@
     for d in range(2):
         z_msg(d, 0, 0, True).wait_recv()
         go(x_msg(d, 1, 0, False))
+    told(0)
+    told(1)
+    tell(2, z_to)
     for d in range(2):
         s = 1 - 2 * d
         y_msg(d, 1, True).wait_recv()
         go(y_msg(d, 4, False))
         go(y_msg(d, 5, False))
         go(z_msg(d, -s, 1, False))
+    told(2)
+    tell(3, z_to)
     for cp in h_in:
         cp.wait()
     for cp in h_out:
@@ -210,16 +220,21 @@
         z_msg(d, 0, 1, True).wait_recv()
         x_msg(d, 1, 0, True).wait_recv()
     mm(piece(1, 0), False, (0, 1))
+    told(3)
+    tell(4, z_to)
     for d in range(2):
         s = 1 - 2 * d
         y_msg(1 - d, 3, True).wait_recv()
         go(z_msg(d, s, 0, False))
         go(x_msg(d, 0, s, False))
+    told(4)
+    tell(5, z_to)
     for d in range(2):
         y_msg(d, 4, True).wait_recv()
         go(z_msg(d, 2, 1, False))
         z_msg(d, 2, 0, True).wait_recv()
         go(x_msg(d, 1, 2, False))
+    told(5)
     for d in range(2):
         s = 1 - 2 * d
         y_msg(1 - d, 5, True).wait_recv()
@@ -461,6 +476,7 @@
             dma((16,)), dma((16,)),
             dma((16,)), dma((16,)),
             dma((16,)), dma((16,)),
+            pltpu.SemaphoreType.REGULAR((6,)),
         ],
         compiler_params=pltpu.CompilerParams(
             collective_id=0, has_side_effects=True, vmem_limit_bytes=56 * 2**20

time: 91.7 us -> 88.2 us (0.962)
  Pallas kernels: 90.3 us -> 86.8 us
    pallas_call x1, Pallas kernels: 88.4 us -> 84.9 us  [local(): pl.pallas_call(kernel, out_shape=(jax.ShapeDtypeStruct((2, 16, 32, 128),...]
where the time goes in v3:
time: 88.2 us; the launch traced here: 88.1 us
  Pallas kernels  86.8 us (98%)
  between operations  1.29 us (1%)
    pallas_call x1, Pallas kernels, local(): pl.pallas_call(kernel, out_shape=(jax.ShapeDtypeStruct((2, 16, 32, 128),...  84.9 us
    pallas_call x1, Pallas kernels, local(): pl.pallas_call(widen, out_shape=(jax.ShapeDtypeStruct((1024, 128), F32),...  1.9 us

profile of v3, /device:TPU:1, one launch (start us, length us, event | category | flops | bytes accessed | tf_op | source)
XLA Modules:
  0.0 88.1 jit_solution(10714701390687593812)
XLA Ops:
  1.3 84.9 %shard_map.86 = (bf16[2,16,32,128]{3,2,1,0:T(8,128)(2,1)}, bf16[2,16,16,128]{3,2,1,0:T(8,128)(2,1)}) custom-call(bf16[1,2,256,8192]{3,2,1,0:T(8,128)(2,1)} %hid.1, bf16[1024,1024]{1,0:T(8,128)(2,1)} %fw.1, bf16[1024,128]{1,0:T(8,128)(2,1)} %ad.1, bf16[2,64,512]{2,1,0:T(8,128)(2,1)} %up_h.1, bf16[1,2,256,512]{3,2,1,0:T(8,128)(2,1)} %ro_h.1, ...), custom_call_target="tpu_custom_call" | custom-call | flops 12000000000 | bytes 12000000 | tf_op jit(solution)/shard_map/pallas_call | solution.py:430
  86.2 1.9 %shard_map.87 = (f32[1024,128]{1,0:T(8,128)}, f32[2,64,512]{2,1,0:T(8,128)}) custom-call(bf16[2,16,32,128]{3,2,1,0:T(8,128)(2,1)} %get-tuple-element.4.gd, bf16[2,16,16,128]{3,2,1,0:T(8,128)(2,1)} %get-tuple-element.5.gu), custom_call_target="tpu_custom_call" | custom-call | flops 1000000 | bytes 2000000 | tf_op jit(solution)/shard_map/pallas_call | solution.py:486

commit v4 on v3

--- a/solution.py
+++ b/solution.py
@@ -340,25 +340,23 @@
         US1[j] = chip[r * 16:(r + 1) * 16, q * 128:(q + 1) * 128].astype(BF16)
 
     def spread16(src, dst, send, recv):
-        def one(k, carry):
+        for k in (10, 9, 11, 8, 6, 14, 5, 13, 7, 15, 4, 12, 2, 1, 3):
             j = (me16 + k) % 16
             rc(src(j), dst.at[me16], send.at[k], recv.at[k], peer16(k)).start()
-            return carry
-        lax.fori_loop(1, 16, one, 0)
 
     def land16(src, dst, send, recv):
         def one(k, carry):
             j = (me16 + 16 - k) % 16
             rc(src(j), dst.at[j], send.at[k], recv.at[k], peer16(k)).wait_recv()
             return carry
-        lax.fori_loop(1, 16, one, 0)
+        lax.fori_loop(1, 16, one, 0, unroll=True)
 
     def sent16(src, dst, send, recv):
         def one(k, carry):
             j = (me16 + k) % 16
             rc(src(j), dst.at[me16], send.at[k], recv.at[k], peer16(k)).wait_send()
             return carry
-        lax.fori_loop(1, 16, one, 0)
+        lax.fori_loop(1, 16, one, 0, unroll=True)
 
     u_args = (lambda j: US1.at[j], US2, vs, vr)
     spread16(*u_args)
@@ -403,10 +401,10 @@
     gd_args = (lambda j: GD.at[c, me16], GD.at[c], gs, gr)
     spread16(*gd_args)
     land16(*gu_args)
+    go(rc(GU.at[c], GU.at[c], ts.at[3], tr.at[3], twin))
     land16(*gd_args)
-    out = [rc(GD.at[c], GD.at[c], ts.at[2], tr.at[2], twin), rc(GU.at[c], GU.at[c], ts.at[3], tr.at[3], twin)]
-    for cp in out:
-        go(cp)
+    out = [rc(GU.at[c], GU.at[c], ts.at[3], tr.at[3], twin), rc(GD.at[c], GD.at[c], ts.at[2], tr.at[2], twin)]
+    go(out[1])
     for cp in out:
         cp.wait_recv()
     for cp in started:

time: 88.2 us -> 86.9 us (0.985)
  Pallas kernels: 86.8 us -> 85.5 us
    pallas_call x1, Pallas kernels: 84.9 us -> 83.6 us  [local(): pl.pallas_call(kernel, out_shape=(jax.ShapeDtypeStruct((2, 16, 32, 128),...]
where the time goes in v4:
time: 86.9 us; the launch traced here: 86.8 us
  Pallas kernels  85.5 us (98%)
  between operations  1.29 us (1%)
    pallas_call x1, Pallas kernels, local(): pl.pallas_call(kernel, out_shape=(jax.ShapeDtypeStruct((2, 16, 32, 128),...  83.6 us
    pallas_call x1, Pallas kernels, local(): pl.pallas_call(widen, out_shape=(jax.ShapeDtypeStruct((1024, 128), F32),...  1.9 us

profile of v4, /device:TPU:1, one launch (start us, length us, event | category | flops | bytes accessed | tf_op | source)
XLA Modules:
  0.0 86.8 jit_solution(12423848477380307986)
XLA Ops:
  1.3 83.6 %shard_map.86 = (bf16[2,16,32,128]{3,2,1,0:T(8,128)(2,1)}, bf16[2,16,16,128]{3,2,1,0:T(8,128)(2,1)}) custom-call(bf16[1,2,256,8192]{3,2,1,0:T(8,128)(2,1)} %hid.1, bf16[1024,1024]{1,0:T(8,128)(2,1)} %fw.1, bf16[1024,128]{1,0:T(8,128)(2,1)} %ad.1, bf16[2,64,512]{2,1,0:T(8,128)(2,1)} %up_h.1, bf16[1,2,256,512]{3,2,1,0:T(8,128)(2,1)} %ro_h.1, ...), custom_call_target="tpu_custom_call" | custom-call | flops 12000000000 | bytes 12000000 | tf_op jit(solution)/shard_map/pallas_call | solution.py:428
  84.9 1.9 %shard_map.87 = (f32[1024,128]{1,0:T(8,128)}, f32[2,64,512]{2,1,0:T(8,128)}) custom-call(bf16[2,16,32,128]{3,2,1,0:T(8,128)(2,1)} %get-tuple-element.4.gd, bf16[2,16,16,128]{3,2,1,0:T(8,128)(2,1)} %get-tuple-element.5.gu), custom_call_target="tpu_custom_call" | custom-call | flops 1000000 | bytes 2000000 | tf_op jit(solution)/shard_map/pallas_call | solution.py:484

commit v5 on v4

--- a/solution.py
+++ b/solution.py
@@ -308,9 +308,9 @@
 
     nt = (((1,), (1,)), ((), ()))
     for i, g in enumerate((gk, gv)):
-        BT[0, pl.ds(i * 64, 64), :] = (adapter_scale * lax.dot_general(
+        BT[pl.ds(i * 64, 64), pl.ds(0, 512)] = (adapter_scale * lax.dot_general(
             up[i], g[...], nt, preferred_element_type=F32)).astype(BF16)
-    b_cp = rc(BT.at[0], BT.at[1], ts.at[0], tr.at[0], twin)
+    b_cp = rc(BT.at[:, pl.ds(0, 512)], BT.at[:, pl.ds(512, 512)], ts.at[0], tr.at[0], twin)
     go(b_cp)
     low_t = jnp.transpose(low[...].astype(F32)).astype(BF16)
     for i, g in enumerate((gk, gv)):
@@ -321,8 +321,7 @@
     b_cp.wait_recv()
 
     def grad(p):
-        own = jnp.dot(BT[0], H[p, pl.ds(0, 2)].reshape(512, 512), preferred_element_type=F32)
-        return own + jnp.dot(BT[1], H[p, pl.ds(2, 2)].reshape(512, 512), preferred_element_type=F32)
+        return jnp.dot(BT[...], H[p].reshape(1024, 512), preferred_element_type=F32)
 
     zd = []
     for dy in (2, 1, 3, 0):
@@ -362,14 +361,13 @@
     spread16(*u_args)
     US2[me16] = US1[me16]
 
-    for dy in (2, 1, 3, 0):
-        E[dy] = grad(piece(0, dy))
     yd = []
     for dy in (2, 1, 3, 0):
+        own = grad(piece(0, dy))
         for dd, cp in zd:
             if dd == dy:
                 cp.wait_recv()
-        t = E[dy] + RZ[dy].astype(F32)
+        t = own + RZ[dy].astype(F32)
         if dy:
             D2[dy] = t.astype(BF16)
             cp = rc(D2.at[dy], RY.at[dy], qs.at[dy], qr.at[dy], at_y(dy))
@@ -446,7 +444,7 @@
             vmem((512, 128), BF16),
             vmem((512, 512), BF16),
             vmem((512, 512), BF16),
-            vmem((2, 128, 512), BF16),
+            vmem((128, 1024), BF16),
             vmem((2, 64, 512), F32),
             vmem((64, 512), F32),
             vmem((16, 16, 128), BF16),

time: 86.9 us -> 87.1 us (level)
  no operation moved by 1% of the time
where the time goes in v5:
time: 87.1 us; the launch traced here: 87 us
  Pallas kernels  85.7 us (98%)
  between operations  1.29 us (1%)
    pallas_call x1, Pallas kernels, local(): pl.pallas_call(kernel, out_shape=(jax.ShapeDtypeStruct((2, 16, 32, 128),...  83.8 us
    pallas_call x1, Pallas kernels, local(): pl.pallas_call(widen, out_shape=(jax.ShapeDtypeStruct((1024, 128), F32),...  1.9 us

profile of v5, /device:TPU:1, one launch (start us, length us, event | category | flops | bytes accessed | tf_op | source)
XLA Modules:
  0.0 87.0 jit_solution(6807319307999095439)
XLA Ops:
  1.3 83.8 %shard_map.86 = (bf16[2,16,32,128]{3,2,1,0:T(8,128)(2,1)}, bf16[2,16,16,128]{3,2,1,0:T(8,128)(2,1)}) custom-call(bf16[1,2,256,8192]{3,2,1,0:T(8,128)(2,1)} %hid.1, bf16[1024,1024]{1,0:T(8,128)(2,1)} %fw.1, bf16[1024,128]{1,0:T(8,128)(2,1)} %ad.1, bf16[2,64,512]{2,1,0:T(8,128)(2,1)} %up_h.1, bf16[1,2,256,512]{3,2,1,0:T(8,128)(2,1)} %ro_h.1, ...), custom_call_target="tpu_custom_call" | custom-call | flops 12000000000 | bytes 12000000 | tf_op jit(solution)/shard_map/pallas_call | solution.py:426
  85.1 1.9 %shard_map.87 = (f32[1024,128]{1,0:T(8,128)}, f32[2,64,512]{2,1,0:T(8,128)}) custom-call(bf16[2,16,32,128]{3,2,1,0:T(8,128)(2,1)} %get-tuple-element.4.gd, bf16[2,16,16,128]{3,2,1,0:T(8,128)(2,1)} %get-tuple-element.5.gu), custom_call_target="tpu_custom_call" | custom-call | flops 1000000 | bytes 2000000 | tf_op jit(solution)/shard_map/pallas_call | solution.py:482
